TPU v7x, 256 devices: a whole 4x4x8 slice. The times are simulated.
256 devices in a mesh: wide: 32 (over y, x, core), narrow: 8 (over z).
Axes of the slice: x: 4, y: 4, z: 8, core: 2. Of those that a mesh axis runs over, the one named last changes fastest.
Arguments:
- queries: bfloat16 [512, 16384], P('wide', 'narrow'), may hold values from -150 to 150
- cache_keys: bfloat16 [512, 256, 1024], P('wide', None, 'narrow'), may hold values from -5 to 5
- cache_values: bfloat16 [512, 256, 1024], P('wide', None, 'narrow'), may hold values from -6 to 6
- new_key: bfloat16 [512, 1024], P('wide', 'narrow'), may hold values from -6 to 6
- new_value: bfloat16 [512, 1024], P('wide', 'narrow'), may hold values from -6 to 6
- lengths: int32 [512], P('wide'), may hold values from 1 to 256, as said below
- out_weight: bfloat16 [16384, 16384], P('narrow', 'wide'), may hold values from -0.046875 to 0.046875
- residual: bfloat16 [512, 16384], P('narrow', 'wide'), may hold values from -30 to 30
- norm_gain: float32 [16384], P('wide'), may hold values from 0.25 to 1.75
- gate_weight: bfloat16 [16384, 26624], P('wide', 'narrow'), may hold values from -0.046875 to 0.046875
- up_weight: bfloat16 [16384, 26624], P('wide', 'narrow'), may hold values from -0.046875 to 0.046875
- down_weight: bfloat16 [26624, 16384], P('narrow', 'wide'), may hold values from -0.0390625 to 0.0390625
Outputs:
- mixed: bfloat16 [512, 16384], P('narrow', 'wide')
Inputs may be any that keep to these rules, and one draw needn't show every extreme that they name: `lengths`: some sequence holds exactly 256 cached tokens.
All inputs are finite; a program needn't handle non-finite values.
Results may differ from a plain program's by a relative error of at most 0.007.
Values may be sent and summed in bfloat16 or wider, within the bound.
A program may use at most 128 MiB of HBM per device.

v0:
```python
import math

import jax
import jax.numpy as jnp
from jax import lax
from jax.sharding import PartitionSpec as P

D = 16384
H = 128
KV = 8
HD = 128


epsilon = 1e-05


def local(
    queries,
    cache_keys,
    cache_values,
    new_key,
    new_value,
    lengths,
    out_weight,
    residual,
    norm_gain,
    gate_weight,
    up_weight,
    down_weight,
):
    group_size = H // KV
    score_scale = 1.0 / math.sqrt(HD)
    seq_count = queries.shape[0]
    cache_len = cache_keys.shape[1]
    local_heads = new_key.shape[1] // HD
    query_rows = queries.reshape(seq_count, local_heads, group_size, HD)
    key_rows = cache_keys.reshape(seq_count, cache_len, local_heads, HD)
    value_rows = cache_values.reshape(seq_count, cache_len, local_heads, HD)
    fresh_key = new_key.reshape(seq_count, local_heads, HD)
    fresh_value = new_value.reshape(seq_count, local_heads, HD)
    scores = (
        jnp.einsum("sgqd,spgd->sgqp", query_rows, key_rows, preferred_element_type=jnp.float32)
        * score_scale
    )
    live_mask = (
        jnp.arange(cache_len, dtype=jnp.int32)[None, None, None, :] < lengths[:, None, None, None]
    )
    own_score = (
        jnp.einsum("sgqd,sgd->sgq", query_rows, fresh_key, preferred_element_type=jnp.float32)
        * score_scale
    )
    row_top = jnp.maximum(jnp.max(jnp.where(live_mask, scores, -1e30), axis=-1), own_score)
    weights_raw = jnp.where(live_mask, jnp.exp(scores - row_top[..., None]), 0.0)
    own_raw = jnp.exp(own_score - row_top)
    row_total = jnp.sum(weights_raw, axis=-1) + own_raw
    weights_bf = (weights_raw / row_total[..., None]).astype(jnp.bfloat16)
    own_bf = (own_raw / row_total).astype(jnp.bfloat16)
    attended = jnp.einsum(
        "sgqp,spgd->sgqd", weights_bf, value_rows, preferred_element_type=jnp.float32
    )
    attended = (
        attended
        + own_bf.astype(jnp.float32)[..., None] * fresh_value.astype(jnp.float32)[:, :, None, :]
    )
    attended = attended.astype(jnp.bfloat16).reshape(seq_count, local_heads * group_size * HD)
    partial_value = jnp.dot(
        lax.all_gather(attended, "wide", axis=0, tiled=True),
        out_weight,
        preferred_element_type=jnp.float32,
    )
    share_rows = residual.shape[0]
    first_row = lax.axis_index("narrow") * share_rows
    own_block = lax.dynamic_slice_in_dim(partial_value, first_row, share_rows, 0) + residual.astype(
        jnp.float32
    )
    partial_value = lax.dynamic_update_slice_in_dim(partial_value, own_block, first_row, 0)
    stream = lax.psum(partial_value, "narrow")
    squares = lax.psum(jnp.sum(stream * stream, axis=1), "wide")
    normed = (stream * lax.rsqrt(squares[:, None] / D + epsilon) * norm_gain).astype(jnp.bfloat16)
    unit_count = gate_weight.shape[1]
    summed = lax.psum_scatter(
        jnp.concatenate(
            [
                jnp.dot(normed, gate_weight, preferred_element_type=jnp.float32),
                jnp.dot(normed, up_weight, preferred_element_type=jnp.float32),
            ],
            axis=1,
        ),
        "wide",
        scatter_dimension=0,
        tiled=True,
    )
    activated = (jax.nn.silu(summed[:, :unit_count]) * summed[:, unit_count:]).astype(jnp.bfloat16)
    branch_terms = jnp.dot(
        lax.all_gather(activated, "wide", axis=0, tiled=True),
        down_weight,
        preferred_element_type=jnp.float32,
    )
    branch_rows = lax.psum_scatter(branch_terms, "narrow", scatter_dimension=0, tiled=True)
    own_rows = lax.dynamic_slice_in_dim(stream, first_row, share_rows, 0)
    return (own_rows + branch_rows).astype(jnp.bfloat16)


def solution(mesh):
    in_specs = (
        P("wide", "narrow"),
        P("wide", None, "narrow"),
        P("wide", None, "narrow"),
        P("wide", "narrow"),
        P("wide", "narrow"),
        P("wide"),
        P("narrow", "wide"),
        P("narrow", "wide"),
        P("wide"),
        P("wide", "narrow"),
        P("wide", "narrow"),
        P("narrow", "wide"),
    )
    out_specs = P("narrow", "wide")
    return jax.shard_map(local, mesh=mesh, in_specs=in_specs, out_specs=out_specs, check_vma=False)
```

profile of v0, /device:TPU:1, one launch (start us, length us, event | category | flops | bytes accessed | tf_op | source)
XLA Modules:
  0.0 431.7 jit_solution(16661763038737199694)
XLA Ops:
  6.5 0.9 iota_compare_fusion
  7.4 0.8 convert_element_type.35
  8.3 0.8 copy.15
  9.1 0.8 fusion.7
  9.9 1.7 select_reduce_fusion
  11.7 0.2 fusion.1
  11.9 1.5 fusion
  13.4 0.7 copy.20
  14.1 0.0 all-gather.3.cloned.1.call-update
  14.1 0.0 all-reduce.2.cloned.1.call-start
  14.2 53.1 %all-gather.3.cloned.1.call-done = bf16[512,2048]{1,0:T(8,128)(2,1)} async-done(((bf16[16,2048]{1,0:T(8,128)(2,1)}), bf16[512,2048]{1,0:T(8,128)(2,1)}) %all-gather.3.cloned.1.call-update) | async-done | bytes 2097168 | tf_op jit(solution)/shard_map/all_gather | solution.py:67
  67.3 4.5 %fusion.14 = f32[512,512]{1,0:T(8,128)} fusion(bf16[512,2048]{1,0:T(8,128)(2,1)} %all-gather.3.cloned.1.call-done, bf16[2048,512]{1,0:T(8,128)(2,1)} %param.18), kind=kOutput, calls=%fused_computation.31 | convolution fusion | flops 1073741824 | bytes 5242880 | tf_op jit(solution)/shard_map/dot_general | solution.py:66
  71.8 1.6 add_dynamic-update-slice_fusion
  73.4 0.0 all-reduce.2.cloned.1.call-update
  73.4 0.0 reduce-scatter.3.cloned.1.call-start
  73.5 70.8 %all-reduce.2.cloned.1.call-done = f32[512,512]{1,0:T(8,128)} async-done(((f32[512,512]{1,0:T(8,128)}), f32[512,512]{1,0:T(8,128)}) %all-reduce.2.cloned.1.call-update) | async-done | bytes 1048592 | tf_op jit(solution)/shard_map/psum | solution.py:77
  144.2 1.4 multiply_reduce_fusion
  145.6 67.1 %psum.15 = f32[512]{0:T(512)S(1)} all-reduce(f32[512]{0:T(512)S(1)} %multiply_reduce_fusion), channel_id=1, replica_groups=mesh['wide'=32,'narrow'=8] {'wide'}, use_global_device_ids=true, to_apply=%region_4.5 | all-reduce | flops 512 | bytes 4096 | tf_op jit(solution)/shard_map/psum | solution.py:78
  212.8 3.4 fusion.12
  216.2 2.0 fusion.13
  218.2 5.5 %pad_maximum_fusion = f32[512,6656]{1,0:T(8,128)} fusion(f32[512,3328]{1,0:T(8,128)S(1)} %fusion.12, f32[512,3328]{1,0:T(8,128)S(1)} %fusion.13), kind=kLoop, calls=%fused_computation | loop fusion | flops 3407872 | bytes 27262976 | tf_op jit(solution)/shard_map/concatenate | solution.py:82
  223.6 0.0 reduce-scatter.3.cloned.1.call-update
  223.6 0.0 all-gather.5.cloned.1.call-start
  223.7 106.9 %reduce-scatter.3.cloned.1.call-done = f32[16,6656]{1,0:T(8,128)} async-done(((f32[512,6656]{1,0:T(8,128)}), f32[16,6656]{1,0:T(8,128)}) %reduce-scatter.3.cloned.1.call-update) | async-done | bytes 426000 | tf_op jit(solution)/shard_map/reduce_scatter | solution.py:81
  330.6 1.8 fusion.2
  332.4 0.0 all-gather.5.cloned.1.call-update
  332.4 0.0 reduce-scatter.5.cloned.1.call-start
  332.4 52.2 %all-gather.5.cloned.1.call-done = bf16[512,3328]{1,0:T(8,128)(2,1)} async-done(((bf16[16,3328]{1,0:T(8,128)(2,1)}), bf16[512,3328]{1,0:T(8,128)(2,1)}) %all-gather.5.cloned.1.call-update) | async-done | bytes 3407888 | tf_op jit(solution)/shard_map/all_gather | solution.py:95
  384.6 5.9 %fusion.15 = f32[512,512]{1,0:T(8,128)} fusion(bf16[512,3328]{1,0:T(8,128)(2,1)} %all-gather.5.cloned.1.call-done, bf16[3328,512]{1,0:T(8,128)(2,1)} %param.23), kind=kOutput, calls=%fused_computation.32 | convolution fusion | flops 1744830464 | bytes 7864320 | tf_op jit(solution)/shard_map/dot_general | solution.py:94
  390.6 0.0 reduce-scatter.5.cloned.1.call-update
  390.6 32.9 %reduce-scatter.5.cloned.1.call-done = f32[64,512]{1,0:T(8,128)} async-done(((f32[512,512]{1,0:T(8,128)}), f32[64,512]{1,0:T(8,128)}) %reduce-scatter.5.cloned.1.call-update) | async-done | bytes 131088 | tf_op jit(solution)/shard_map/reduce_scatter | solution.py:99
  423.5 1.6 add_convert_fusion
  (14 shorter events, 0.1 us)
Async XLA Ops:
  6.5 206.2 %copy-start = (bf16[512,3328]{1,0:T(8,128)(2,1)S(1)}, bf16[512,3328]{1,0:T(8,128)(2,1)}, u32[]{:S(2)}) copy-start(bf16[512,3328]{1,0:T(8,128)(2,1)} %param.22) | copy-start | bytes 10223620
  6.5 60.8 %all-gather.3.cloned.1.call-start = ((), (), s32[]{:S(2)}) async-start(), calls=%async_computation.2 | async-start | bytes 2162688 | tf_op jit(solution)/shard_map/all_gather | solution.py:67
  14.1 130.1 %all-reduce.2.cloned.1.call-start = ((), (), s32[]{:S(2)}) async-start(), calls=%async_computation.3 | async-start | bytes 2097152 | tf_op jit(solution)/shard_map/psum | solution.py:77
  14.2 57.6 %copy-start.4 = (bf16[64,512]{1,0:T(8,128)(2,1)S(1)}, bf16[64,512]{1,0:T(8,128)(2,1)}, u32[]{:S(2)}) copy-start(bf16[64,512]{1,0:T(8,128)(2,1)} %param.19) | copy-start | bytes 196612
  14.2 198.6 %copy-start.3 = (f32[512]{0:T(512)S(1)}, f32[512]{0:T(512)}, u32[]{:S(2)}) copy-start(f32[512]{0:T(512)} %param.20) | copy-start | bytes 6148
  73.4 257.2 %reduce-scatter.3.cloned.1.call-start = ((), (), s32[]{:S(2)}) async-start(), calls=%async_computation.4 | async-start | bytes 14057472 | tf_op jit(solution)/shard_map/reduce_scatter | solution.py:81
  212.8 3.4 copy-start.1
  212.8 3.4 copy-start.2
  223.6 161.0 %all-gather.5.cloned.1.call-start = ((), (), s32[]{:S(2)}) async-start(), calls=%async_computation.5 | async-start | bytes 3514368 | tf_op jit(solution)/shard_map/all_gather | solution.py:95
  332.4 91.1 %reduce-scatter.5.cloned.1.call-start = ((), (), s32[]{:S(2)}) async-start(), calls=%async_computation.6 | async-start | bytes 1179648 | tf_op jit(solution)/shard_map/reduce_scatter | solution.py:99
Sparse Core Ops, SparseCore 0:
  14.2 53.0 all-gather.2
  73.5 70.6 all-reduce.1
  223.8 106.7 reduce-scatter.2
  333.3 51.2 all-gather.4
  390.7 32.7 reduce-scatter.4
where the time goes:
time: 436 us; the launch traced here: 432 us
  waiting for transfers between devices  316 us (72%)
  blocking collectives  67.1 us (15%)
  matrix products  19.8 us (5%)
  other arithmetic  13.8 us (3%)
  between operations  13.2 us (3%)
    reduce_scatter x1, waiting for transfers between devices, local(): lax.psum_scatter(jnp.concatenate([jnp.dot(normed, gate_weight, preferred_...  107 us
    psum x1, waiting for transfers between devices, local(): stream = lax.psum(partial_value, 'narrow')  70.8 us
    psum x1, blocking collectives, local(): squares = lax.psum(jnp.sum(stream * stream, axis=1), 'wide')  67.1 us
    all_gather x1, waiting for transfers between devices, local(): lax.all_gather(attended, 'wide', axis=0, tiled=True)  53.1 us
    all_gather x1, waiting for transfers between devices, local(): lax.all_gather(activated, 'wide', axis=0, tiled=True)  52.2 us
    reduce_scatter x1, waiting for transfers between devices, local(): lax.psum_scatter(branch_terms, 'narrow', scatter_dimension=0, tiled=True)  32.9 us
  transfers between devices with their start and end apart: 5, of which 5 were waited for; matrix products, arithmetic and copies ran while one was open for 0% of the time, Pallas kernels for 0%

commit v1 on v0

v1 whole, which is shorter than its diff:
```python
import functools
import math

import jax
import jax.numpy as jnp
from jax import lax
from jax.experimental import pallas as pl
from jax.experimental.pallas import tpu as pltpu
from jax.sharding import PartitionSpec as P

D = 16384
HD = 128
EPS = 1e-05
NX, NY, NZ = 4, 4, 8
STREAMS = 2
MESH = pl.DeviceIdType.MESH
F32 = jnp.float32
BF16 = jnp.bfloat16


def body(
    len_ref, q_hbm, nk_hbm, nv_hbm, res_hbm, gain_hbm,
    k_hbm, v_hbm, wo_hbm, wg_hbm, wu_hbm, wd_hbm,
    out_ref,
    q_ref, nk_ref, nv_ref, res_ref, gain_ref, kv, vv, wo, wg, wu, wd, gain_sib, qs, ao, ps, pr, ag, po, cs, cr, zs, zr, st,
    xn, sq, gs, gr, gp, gr2, ac, fin,
    lsem, wss, wrs, d2s, d2r, p4s, p4r, zss, zrs,
):
    w = lax.axis_index("wide")
    z = lax.axis_index("narrow")
    c = lax.rem(w, 2)
    chip = lax.div(w, 2)
    x = lax.rem(chip, NX)
    y = lax.div(chip, NX)
    units = wg.shape[1]
    depth = wg.shape[0] // 2

    sibling = (chip * 2 + (1 - c), z)

    p = jnp.where(c == 0, x, y)
    q = jnp.where(c == 0, y, x)

    def natural(second, first):
        return jnp.where(c == 0, second * NX + first, first * NX + second)

    def ppeer(d):
        return lax.rem(p + d, NX)

    def qpeer(d):
        return lax.rem(q + d, NX)

    def zpeer(d):
        return lax.rem(z + d, NZ)

    def pdev(d):
        return (natural(q, ppeer(d)) * 2 + c, z)

    def qdev(d):
        return (natural(qpeer(d), p) * 2 + c, z)

    def zdev(d):
        return (w, zpeer(d))

    barrier = pltpu.get_barrier_semaphore()
    peers = [sibling] + [pdev(d) for d in (1, 2, 3)] + [qdev(d) for d in (1, 2, 3)]
    peers += [zdev(d) for d in range(1, NZ)]
    for dev in peers:
        pl.semaphore_signal(barrier, inc=1, device_id=dev, device_id_type=MESH)

    sent = []
    drained = []

    def send(src, dst, ss, rs, dev):
        copy = pltpu.make_async_remote_copy(
            src_ref=src, dst_ref=dst, send_sem=ss, recv_sem=rs, device_id=dev, device_id_type=MESH
        )
        copy.start()
        sent.append(copy)
        return copy

    def drain(count):
        while len(drained) < count:
            copy = sent[len(drained)]
            copy.wait_send()
            drained.append(copy)

    k_rows = wo.shape[1]
    f_rows = wd.shape[1]
    d_cols = pl.ds(pl.multiple_of(c * units, 128), units)
    d_cols_sib = pl.ds(pl.multiple_of((1 - c) * units, 128), units)
    half = kv.shape[0] // STREAMS
    small = [
        pltpu.make_async_copy(src, dst, lsem.at[8 + i])
        for i, (src, dst) in enumerate((
            (q_hbm, q_ref), (nk_hbm, nk_ref), (nv_hbm, nv_ref), (res_hbm, res_ref),
            (gain_hbm, gain_ref),
        ))
    ]
    loads = []
    for s in range(STREAMS):
        rows = pl.ds(s * half, half)
        loads.append(pltpu.make_async_copy(k_hbm.at[rows], kv.at[rows], lsem.at[2 * s]))
        loads.append(pltpu.make_async_copy(v_hbm.at[rows], vv.at[rows], lsem.at[2 * s + 1]))
    own_rows = pl.ds(pl.multiple_of(c * k_rows, 128), k_rows)
    sib_rows = pl.ds(pl.multiple_of((1 - c) * k_rows, 128), k_rows)
    own_units = pl.ds(pl.multiple_of(c * f_rows, 128), f_rows)
    sib_units = pl.ds(pl.multiple_of((1 - c) * f_rows, 128), f_rows)
    load_wo = pltpu.make_async_copy(wo_hbm.at[own_rows], wo.at[0], lsem.at[4])
    load_wg = pltpu.make_async_copy(wg_hbm.at[:, d_cols], wg.at[0:depth], lsem.at[5])
    load_wu = pltpu.make_async_copy(wu_hbm.at[:, d_cols], wu.at[0:depth], lsem.at[6])
    load_wd = pltpu.make_async_copy(wd_hbm.at[own_units], wd.at[0], lsem.at[7])
    for copy in small + loads + [load_wo, load_wg, load_wu, load_wd]:
        copy.start()

    for copy in small:
        copy.wait()
    heads = q_ref.shape[1] // HD
    seqs = q_ref.shape[0]
    for h in range(heads):
        qs[pl.ds(h, seqs, stride=heads), :] = q_ref[:, h * HD:(h + 1) * HD].astype(F32)

    scale = 1.0 / math.sqrt(HD)

    def attend(s):
        loads[2 * s].wait()
        loads[2 * s + 1].wait()
        ctx = kv.shape[1]
        position = lax.broadcasted_iota(jnp.int32, (heads, ctx), 1)
        items = range(half)
        seq = [s * half + i for i in items]
        query = [qs[n * heads:(n + 1) * heads, :] for n in seq]
        score = [
            lax.dot_general(
                query[i].astype(BF16), kv[seq[i]], (((1,), (1,)), ((), ())),
                preferred_element_type=F32,
            )
            for i in items
        ]
        own = [
            jnp.sum(query[i] * nk_ref[n:n + 1, :].astype(F32), axis=1, keepdims=True) * scale
            for i, n in enumerate(seq)
        ]
        live = [position < len_ref[n] for n in seq]
        score = [jnp.where(live[i], score[i] * scale, -1e30) for i in items]
        top = [jnp.maximum(jnp.max(score[i], axis=1, keepdims=True), own[i]) for i in items]
        raw = [jnp.where(live[i], jnp.exp(score[i] - top[i]), 0.0) for i in items]
        own_raw = [jnp.exp(own[i] - top[i]) for i in items]
        inverse = [1.0 / (jnp.sum(raw[i], axis=1, keepdims=True) + own_raw[i]) for i in items]
        weights = [(raw[i] * inverse[i]).astype(BF16) for i in items]
        own_weight = [(own_raw[i] * inverse[i]).astype(BF16).astype(F32) for i in items]
        mixed = [jnp.dot(weights[i], vv[seq[i]], preferred_element_type=F32) for i in items]
        for i, n in enumerate(seq):
            ao[s, i * heads:(i + 1) * heads, :] = (
                mixed[i] + own_weight[i] * nv_ref[n:n + 1, :].astype(F32)
            )

    per_core = heads // 2

    def swap_start(s):
        for h in range(per_core):
            cols = slice(h * HD, (h + 1) * HD)
            ps[s, 0, :, cols] = ao[s, pl.ds(c * per_core + h, half, stride=heads), :]
            ps[s, 1, :, cols] = ao[s, pl.ds((1 - c) * per_core + h, half, stride=heads), :]
        return send(ps.at[s, 1], pr.at[s], d2s.at[s, 0], d2r.at[s, 0], sibling)

    def gather_first(s, k, buf):
        return [
            send(buf.at[s, q, p], buf.at[s, q, p], p4s.at[s, k, d - 1], p4r.at[s, k, d - 1], pdev(d))
            for d in (2, 1, 3)
        ]

    def gather_second(s, k, buf):
        return [
            send(buf.at[s, q], buf.at[s, q], p4s.at[s, k, d - 1], p4r.at[s, k, d - 1], qdev(d))
            for d in (2, 1, 3)
        ]

    def arrive(copies):
        for copy in copies:
            copy.wait_recv()

    def swap_end_gather(s, copy):
        copy.wait_recv()
        mine = ps[s, 0]
        theirs = pr[s]
        first = jnp.where(c == 0, mine, theirs)
        second = jnp.where(c == 0, theirs, mine)
        block = jnp.concatenate([first, second], axis=0).astype(BF16)
        ag[s, q, p] = block
        return gather_first(s, 0, ag)

    rows = NX * NY * 16

    def project(s, k, buf, weight):
        depth_here = buf.shape[-1]
        for half_index in (1, 0):
            for n in range(weight.shape[-1] // 256):
                cols = slice(n * 256, (n + 1) * 256)
                acc = jnp.dot(buf[s].reshape(rows, depth_here), weight[half_index, :, cols],
                              preferred_element_type=F32)
                for a in range(NY):
                    for b in range(NX):
                        r = (a * NX + b) * 16
                        to = pl.ds(pl.multiple_of(natural(a, b) * 16, 16), 16)
                        if half_index:
                            cs[s, k, to, cols] = acc[r:r + 16].astype(BF16)
                        else:
                            po[s, k, to, cols] = acc[r:r + 16]
            if half_index:
                copy = send(cs.at[s, k], cr.at[s, k], d2s.at[s, 1 + k], d2r.at[s, 1 + k], sibling)
        return copy

    share = rows // NZ

    def scatter_z(s, k, copy):
        copy.wait_recv()
        for j in range(NZ):
            r = slice(j * share, (j + 1) * share)
            zs[s, k, j] = (po[s, k, r, :] + cr[s, k, r, :].astype(F32)).astype(BF16)
        out = []
        for d in (4, 3, 5, 2, 6, 1, 7):
            out.append(send(zs.at[s, k, zpeer(d)], zr.at[s, k, d - 1],
                            zss.at[s, k, d - 1], zrs.at[s, k, d - 1], zdev(d)))
        return out

    def sum_z(s, k, copies):
        own = pl.ds(pl.multiple_of(z * share, share), share)
        acc = po[s, k, own, :] + cr[s, k, own, :].astype(F32)
        arrive(copies)
        for d in range(1, NZ):
            acc += zr[s, k, d - 1].astype(F32)
        return acc

    def norm_gather(s, copies):
        stream = sum_z(s, 0, copies)
        pieces = [
            res_ref[g * 16:(g + 1) * 16, :].astype(F32)[s * 8:(s + 1) * 8] for g in range(share // 8)
        ]
        stream = stream + jnp.concatenate(pieces, axis=0)
        st[s] = stream
        xn[s, z, :, 0:depth] = (stream * gain_ref[...]).astype(BF16)
        out = []
        for d in (4, 3, 5, 2, 6, 1, 7):
            out.append(send(xn.at[s, z, :, 0:depth], xn.at[s, z, :, 0:depth],
                            zss.at[s, 2, d - 1], zrs.at[s, 2, d - 1], zdev(d)))
        return out

    def encode(value):
        high = value.astype(BF16).astype(F32)
        lane = lax.broadcasted_iota(jnp.int32, value.shape, 1)
        return jnp.where(lane < 64, high, value - high).astype(BF16)

    def decode(pair):
        value = pair.astype(F32)
        return value + pltpu.roll(value, 64, 1)

    def row_squares(s, first):
        gain = gain_sib if first else gain_ref
        ungain = 1.0 / gain[...]
        for j in range(NZ):
            value = xn[s, j, :, first:first + depth].astype(F32) * ungain
            value = value * value
            total = value[:, 0:128]
            for n in range(1, depth // 128):
                total += value[:, n * 128:(n + 1) * 128]
            r = slice(j * share, (j + 1) * share)
            if first:
                total += sq[r, :]
                total = jnp.broadcast_to(jnp.sum(total, axis=1, keepdims=True), (share, 128))
            sq[r, :] = total

    def swap_normed(s, copies):
        arrive(copies)
        return send(xn.at[s, :, :, 0:depth], xn.at[s, :, :, depth:2 * depth],
                    d2s.at[s, 3], d2r.at[s, 3], sibling)

    def spread(s, cols, value):
        for j in range(NY):
            for i in range(NX):
                r = (j * NX + i) * 16
                first = jnp.where(c == 0, i, j)
                second = jnp.where(c == 0, j, i)
                gs[s, first, second, :, cols] = value[r:r + 16]

    def expand(s, copy):
        row_squares(s, 0)
        copy.wait_recv()
        row_squares(s, depth)
        spread(s, slice(2 * units, 2 * units + 128), encode(sq[...]))
        for k, weight in enumerate((wg, wu)):
            for start in range(0, units, 256):
                size = min(256, units - start)
                acc = jnp.dot(xn[s].reshape(rows, 2 * depth), weight[:, start:start + size],
                              preferred_element_type=F32)
                base = k * units + start
                spread(s, slice(base, base + size), acc.astype(BF16))
        return [
            send(gs.at[s, ppeer(d)], gr.at[s, d - 1], p4s.at[s, 2, d - 1], p4r.at[s, 2, d - 1],
                 pdev(d))
            for d in (2, 1, 3)
        ]

    def sum_second(s, copies):
        arrive(copies)

        def block(j, _):
            acc = gs[s, p, j, :, 0:2 * units].astype(F32)
            square = decode(gs[s, p, j, :, 2 * units:])
            for d in range(3):
                acc += gr[s, d, j, :, 0:2 * units].astype(F32)
                square += decode(gr[s, d, j, :, 2 * units:])
            gp[s, j, :, 0:2 * units] = acc.astype(BF16)
            gp[s, j, :, 2 * units:] = encode(square)
            return 0
        lax.fori_loop(0, NY, block, 0)
        return [
            send(gp.at[s, qpeer(d)], gr2.at[s, d - 1], p4s.at[s, 3, d - 1], p4r.at[s, 3, d - 1],
                 qdev(d))
            for d in (2, 1, 3)
        ]

    def activate(s, copies):
        arrive(copies)
        square = decode(gp[s, q, :, 2 * units:])
        for d in range(3):
            square += decode(gr2[s, d, :, 2 * units:])
        factor = lax.rsqrt(square / D + EPS)
        for n in range(units // 128):
            cols = slice(n * 128, (n + 1) * 128)
            lift_cols = slice(units + n * 128, units + (n + 1) * 128)
            gate = gp[s, q, :, cols].astype(F32)
            lift = gp[s, q, :, lift_cols].astype(F32)
            for d in range(3):
                gate += gr2[s, d, :, cols].astype(F32)
                lift += gr2[s, d, :, lift_cols].astype(F32)
            gate = gate * factor
            ac[s, q, p, :, cols] = (
                gate / (1.0 + jnp.exp(-gate)) * (lift * factor)
            ).astype(BF16)
        return gather_first(s, 4, ac)

    S = range(STREAMS)
    for s in S:
        attend(s)
    pl.semaphore_wait(barrier, len(peers))
    swaps = [swap_start(s) for s in S]
    share_gain = send(gain_hbm, gain_sib, wss.at[4], wrs.at[4], sibling)
    share_wo = send(wo_hbm.at[sib_rows], wo.at[1], wss.at[0], wrs.at[0], sibling)
    a1 = [swap_end_gather(s, swaps[s]) for s in S]
    share_wg = send(wg_hbm.at[:, d_cols_sib], wg.at[depth:2 * depth], wss.at[1], wrs.at[1], sibling)
    share_wu = send(wu_hbm.at[:, d_cols_sib], wu.at[depth:2 * depth], wss.at[2], wrs.at[2], sibling)
    a2 = []
    for s in S:
        arrive(a1[s])
        a2.append(gather_second(s, 1, ag))
    load_wo.wait()
    share_wo.wait_recv()
    r1 = []
    for s in S:
        arrive(a2[s])
        c1 = project(s, 0, ag, wo)
        r1.append(scatter_z(s, 0, c1))
    share_wd = send(wd_hbm.at[sib_units], wd.at[1], wss.at[3], wrs.at[3], sibling)
    for copy in (load_wg, load_wu, load_wd):
        copy.wait()
    for copy in (share_gain, share_wg, share_wu):
        copy.wait_recv()
    drain(16)
    n1 = [norm_gather(s, r1[s]) for s in S]
    drain(32)
    share_wd.wait_recv()
    e1 = []
    for s in S:
        e1.append(expand(s, swap_normed(s, n1[s])))
    drain(48)
    e2 = [sum_second(0, e1[0])]
    b1 = [activate(0, e2[0])]
    e2.append(sum_second(1, e1[1]))
    arrive(b1[0])
    b2 = [gather_second(0, 5, ac)]
    b1.append(activate(1, e2[1]))
    arrive(b2[0])
    c2 = project(0, 1, ac, wd)
    arrive(b1[1])
    b2.append(gather_second(1, 5, ac))
    r2 = [scatter_z(0, 1, c2)]
    drain(len(sent) - 24)
    arrive(b2[1])
    c2 = project(1, 1, ac, wd)
    r2.append(scatter_z(1, 1, c2))
    drain(len(sent) - 9)
    for s in S:
        fin[s] = st[s] + sum_z(s, 1, r2[s])
    for g in range(share // 8):
        out_ref[g * 16:(g + 1) * 16, :] = jnp.concatenate(
            [fin[s, g * 8:(g + 1) * 8, :] for s in S], axis=0
        ).astype(BF16)
    drain(len(sent))


def local(
    queries, cache_keys, cache_values, new_key, new_value, lengths,
    out_weight, residual, norm_gain, gate_weight, up_weight, down_weight,
):
    seqs, ctx, _ = cache_keys.shape
    heads = queries.shape[1] // HD
    half = seqs // STREAMS
    kh = out_weight.shape[0] // 2
    cols = out_weight.shape[1]
    depth, hidden = gate_weight.shape
    units = hidden // 2
    wide_row = 2 * units + 128
    rows = NX * NY * 2 * half
    share = rows // NZ
    S = STREAMS
    DMA = pltpu.SemaphoreType.DMA

    def v(*shape, dtype=BF16):
        return pltpu.VMEM(shape, dtype)

    scratch = [
        v(*queries.shape), v(*new_key.shape), v(*new_value.shape), v(*residual.shape),
        v(1, cols, dtype=F32),
        v(seqs, ctx, HD), v(seqs, ctx, HD),
        v(2, kh, cols), v(2 * depth, units), v(2 * depth, units), v(2, units, cols),
        v(1, cols, dtype=F32),
        v(seqs * heads, HD, dtype=F32),
        v(S, half * heads, HD, dtype=F32),
        v(S, 2, half, kh, dtype=F32), v(S, half, kh, dtype=F32),
        v(S, NY, NX, 16, kh),
        v(S, 2, rows, cols, dtype=F32),
        v(S, 2, rows, cols), v(S, 2, rows, cols),
        v(S, 2, NZ, share, cols), v(S, 2, NZ - 1, share, cols),
        v(S, share, cols, dtype=F32),
        v(S, NZ, share, 2 * depth), v(rows, 128, dtype=F32),
        v(S, NX, NY, 16, wide_row), v(S, 3, NY, 16, wide_row),
        v(S, NY, 16, wide_row), v(S, 3, 16, wide_row),
        v(S, NY, NX, 16, units),
        v(S, share, cols, dtype=F32),
        DMA((13,)), DMA((5,)), DMA((5,)),
        DMA((S, 4)), DMA((S, 4)),
        DMA((S, 6, 3)), DMA((S, 6, 3)),
        DMA((S, 3, NZ - 1)), DMA((S, 3, NZ - 1)),
    ]
    vm = pl.BlockSpec(memory_space=pltpu.VMEM)
    hbm = pl.BlockSpec(memory_space=pl.ANY)
    return pl.pallas_call(
        body,
        out_shape=jax.ShapeDtypeStruct(residual.shape, BF16),
        in_specs=[pl.BlockSpec(memory_space=pltpu.SMEM)] + [hbm] * 11,
        out_specs=vm,
        scratch_shapes=scratch,
        compiler_params=pltpu.CompilerParams(
            collective_id=0, has_side_effects=True, vmem_limit_bytes=58 << 20
        ),
        name="layer",
    )(
        lengths, queries, new_key, new_value, residual, norm_gain.reshape(1, -1),
        cache_keys, cache_values, out_weight, gate_weight, up_weight, down_weight,
    )


def solution(mesh):
    in_specs = (
        P("wide", "narrow"),
        P("wide", None, "narrow"),
        P("wide", None, "narrow"),
        P("wide", "narrow"),
        P("wide", "narrow"),
        P("wide"),
        P("narrow", "wide"),
        P("narrow", "wide"),
        P("wide"),
        P("wide", "narrow"),
        P("wide", "narrow"),
        P("narrow", "wide"),
    )
    out_specs = P("narrow", "wide")
    return jax.shard_map(local, mesh=mesh, in_specs=in_specs, out_specs=out_specs, check_vma=False)
```

time: 436 us -> 104 us (0.24)
  waiting for transfers between devices: 316 us -> 0 us
  Pallas kernels: 0 us -> 102 us
  blocking collectives: 67.1 us -> 0 us
  matrix products: 19.8 us -> 0 us
  other arithmetic: 13.8 us -> 0 us
  between operations: 13.2 us -> 0.01 us
    reduce_scatter x2 -> x0, waiting for transfers between devices: 140 us -> none  [the longest x1 107 us: local(): lax.psum_scatter(jnp.concatenate([jnp.dot(normed, gate_weight, preferred_...]
    all_gather x2 -> x0, waiting for transfers between devices: 105 us -> none  [the longest x1 53.1 us: local(): lax.all_gather(attended, 'wide', axis=0, tiled=True)]
    pallas_call x0 -> x1, Pallas kernels: none -> 102 us  [local(): pl.pallas_call(body, out_shape=jax.ShapeDtypeStruct(residual.shape, BF16)...]
    psum x1 -> x0, waiting for transfers between devices: 70.8 us -> none  [local(): stream = lax.psum(partial_value, 'narrow')]
    psum x1 -> x0, blocking collectives: 67.1 us -> none  [local(): squares = lax.psum(jnp.sum(stream * stream, axis=1), 'wide')]
    dot_general x7 -> x0, matrix products: 19.8 us -> none  [the longest x1 5.93 us: local(): jnp.dot(lax.all_gather(activated, 'wide', axis=0, tiled=True), down_weigh...]
    concatenate x1 -> x0, other arithmetic: 5.46 us -> none  [local(): jnp.concatenate([jnp.dot(normed, gate_weight, preferred_element_type=jnp....]
  transfers between devices with their start and end apart: 5 -> 0, of which waited for: 5 -> 0; matrix products, arithmetic and copies ran while one was open for 0% -> 0% of each run, Pallas kernels for 0% -> 0%
where the time goes in v1:
time: 104 us
  Pallas kernels  102 us (98%)
  local copies, waits for them, and re-layouts  1.47 us (1%)
    pallas_call x1, Pallas kernels, local(): pl.pallas_call(body, out_shape=jax.ShapeDtypeStruct(residual.shape, BF16)...  102 us

profile of v1, /device:TPU:1, one launch (start us, length us, event | category | flops | bytes accessed | tf_op | source)
XLA Modules:
  0.0 103.7 jit_solution(922746260226749113)
XLA Ops:
  0.0 102.2 %layer.1 = bf16[64,512]{1,0:T(8,128)(2,1)} custom-call(s32[16]{0:T(128)} %len_ref.1, bf16[16,2048]{1,0:T(8,128)(2,1)} %q_hbm.1, bf16[16,128]{1,0:T(8,128)(2,1)} %nk_hbm.1, bf16[16,128]{1,0:T(8,128)(2,1)} %nv_hbm.1, bf16[64,512]{1,0:T(8,128)(2,1)} %res_hbm.1, f32[1,512]{1,0:T(1,128)} %bitcast.1, bf16[16,256,128]{2,1,0:T(8,128)(2,1)} %k_hbm.1, ...), custom_call_target="tpu_custom_call" | custom-call | tf_op jit(solution)/shard_map/layer/pallas_call | solution.py:447
  102.2 1.5 %copy.14 = bf16[64,512]{1,0:T(8,128)(2,1)} copy(bf16[64,512]{1,0:T(8,128)(2,1)} %layer.1) | data formatting | bytes 131072

commit v2 on v1

--- a/solution.py
+++ b/solution.py
@@ -22,7 +22,7 @@
     len_ref, q_hbm, nk_hbm, nv_hbm, res_hbm, gain_hbm,
     k_hbm, v_hbm, wo_hbm, wg_hbm, wu_hbm, wd_hbm,
     out_ref,
-    q_ref, nk_ref, nv_ref, res_ref, gain_ref, kv, vv, wo, wg, wu, wd, gain_sib, qs, ao, ps, pr, ag, po, cs, cr, zs, zr, st,
+    q_ref, nk_ref, nv_ref, res_ref, gain_ref, kv, vv, wo, wg, wu, wd, gain_sib, qs, ao, ps, pr, ag, po, cs, cr, zs, zr, zt, st,
     xn, sq, gs, gr, gp, gr2, ac, fin,
     lsem, wss, wrs, d2s, d2r, p4s, p4r, zss, zrs,
 ):
@@ -212,23 +212,45 @@
 
     share = rows // NZ
 
+    top, bottom = slice(0, share // 2), slice(share // 2, share)
+
+    def zsend(s, k, i, src, dst, d):
+        return send(src, dst, zss.at[s, k, i], zrs.at[s, k, i], zdev(d))
+
     def scatter_z(s, k, copy):
         copy.wait_recv()
         for j in range(NZ):
             r = slice(j * share, (j + 1) * share)
             zs[s, k, j] = (po[s, k, r, :] + cr[s, k, r, :].astype(F32)).astype(BF16)
-        out = []
-        for d in (4, 3, 5, 2, 6, 1, 7):
-            out.append(send(zs.at[s, k, zpeer(d)], zr.at[s, k, d - 1],
-                            zss.at[s, k, d - 1], zrs.at[s, k, d - 1], zdev(d)))
-        return out
+        src = [zs.at[s, k, zpeer(d)] for d in range(NZ)]
+        return [
+            zsend(s, k, 0, src[4].at[top], zr.at[s, k, 0, top], 2),
+            zsend(s, k, 1, src[4].at[bottom], zr.at[s, k, 1, bottom], 6),
+            zsend(s, k, 2, src[3], zr.at[s, k, 2], 1),
+            zsend(s, k, 3, src[5], zr.at[s, k, 3], 7),
+            zsend(s, k, 4, src[1], zr.at[s, k, 4], 1),
+            zsend(s, k, 5, src[7], zr.at[s, k, 5], 7),
+        ]
+
+    def relay_z(s, k, copies):
+        for i, (part, d) in enumerate(((top, 2), (bottom, 6))):
+            copies[i].wait_recv()
+            copies[2 + i].wait_recv()
+            to = zpeer(d)
+            zt[s, k, i] = (zs[s, k, to].astype(F32) + zr[s, k, 2 + i].astype(F32)).astype(BF16)
+            zt[s, k, i, part] = (
+                zs[s, k, to, part].astype(F32) + zr[s, k, 2 + i, part].astype(F32)
+                + zr[s, k, i, part].astype(F32)
+            ).astype(BF16)
+            copies.append(zsend(s, k, 6 + i, zt.at[s, k, i], zr.at[s, k, 6 + i], d))
+        return copies[4:]
 
     def sum_z(s, k, copies):
         own = pl.ds(pl.multiple_of(z * share, share), share)
         acc = po[s, k, own, :] + cr[s, k, own, :].astype(F32)
         arrive(copies)
-        for d in range(1, NZ):
-            acc += zr[s, k, d - 1].astype(F32)
+        for i in range(4, 8):
+            acc += zr[s, k, i].astype(F32)
         return acc
 
     def norm_gather(s, copies):
@@ -239,11 +261,18 @@
         stream = stream + jnp.concatenate(pieces, axis=0)
         st[s] = stream
         xn[s, z, :, 0:depth] = (stream * gain_ref[...]).astype(BF16)
-        out = []
-        for d in (4, 3, 5, 2, 6, 1, 7):
-            out.append(send(xn.at[s, z, :, 0:depth], xn.at[s, z, :, 0:depth],
-                            zss.at[s, 2, d - 1], zrs.at[s, 2, d - 1], zdev(d)))
-        return out
+        block = xn.at[s, z, :, 0:depth]
+        return [zsend(s, 2, i, block, block, d) for i, d in enumerate((2, 6, 1, 7))]
+
+    def relay_normed(s, copies):
+        for i, (part, near, far) in enumerate(((top, 1, 2), (bottom, 7, 6))):
+            copies[i].wait_recv()
+            came = zpeer(NZ - far)
+            half_block = xn.at[s, came, part, 0:depth]
+            block = xn.at[s, came, :, 0:depth]
+            copies.append(zsend(s, 2, 4 + 2 * i, half_block, half_block, far))
+            copies.append(zsend(s, 2, 5 + 2 * i, block, block, near))
+        return copies[2:]
 
     def encode(value):
         high = value.astype(BF16).astype(F32)
@@ -366,7 +395,9 @@
     for copy in (share_gain, share_wg, share_wu):
         copy.wait_recv()
     drain(16)
+    r1 = [relay_z(s, 0, r1[s]) for s in S]
     n1 = [norm_gather(s, r1[s]) for s in S]
+    n1 = [relay_normed(s, n1[s]) for s in S]
     drain(32)
     share_wd.wait_recv()
     e1 = []
@@ -387,8 +418,10 @@
     drain(len(sent) - 24)
     arrive(b2[1])
     c2 = project(1, 1, ac, wd)
+    r2[0] = relay_z(0, 1, r2[0])
     r2.append(scatter_z(1, 1, c2))
-    drain(len(sent) - 9)
+    drain(len(sent) - 16)
+    r2[1] = relay_z(1, 1, r2[1])
     for s in S:
         fin[s] = st[s] + sum_z(s, 1, r2[s])
     for g in range(share // 8):
@@ -430,7 +463,8 @@
         v(S, NY, NX, 16, kh),
         v(S, 2, rows, cols, dtype=F32),
         v(S, 2, rows, cols), v(S, 2, rows, cols),
-        v(S, 2, NZ, share, cols), v(S, 2, NZ - 1, share, cols),
+        v(S, 2, NZ, share, cols), v(S, 2, 8, share, cols),
+        v(S, 2, 2, share, cols),
         v(S, share, cols, dtype=F32),
         v(S, NZ, share, 2 * depth), v(rows, 128, dtype=F32),
         v(S, NX, NY, 16, wide_row), v(S, 3, NY, 16, wide_row),
@@ -440,7 +474,7 @@
         DMA((13,)), DMA((5,)), DMA((5,)),
         DMA((S, 4)), DMA((S, 4)),
         DMA((S, 6, 3)), DMA((S, 6, 3)),
-        DMA((S, 3, NZ - 1)), DMA((S, 3, NZ - 1)),
+        DMA((S, 3, 8)), DMA((S, 3, 8)),
     ]
     vm = pl.BlockSpec(memory_space=pltpu.VMEM)
     hbm = pl.BlockSpec(memory_space=pl.ANY)

time: 104 us -> 99.6 us (0.958)
  Pallas kernels: 102 us -> 98 us
    pallas_call x1, Pallas kernels: 102 us -> 98 us  [local(): pl.pallas_call(body, out_shape=jax.ShapeDtypeStruct(residual.shape, BF16)...]
where the time goes in v2:
time: 99.6 us; the launch traced here: 99.5 us
  Pallas kernels  98 us (98%)
  local copies, waits for them, and re-layouts  1.47 us (1%)
    pallas_call x1, Pallas kernels, local(): pl.pallas_call(body, out_shape=jax.ShapeDtypeStruct(residual.shape, BF16)...  98 us

profile of v2, /device:TPU:1, one launch (start us, length us, event | category | flops | bytes accessed | tf_op | source)
XLA Modules:
  0.0 99.5 jit_solution(10266562574859749731)
XLA Ops:
  0.0 98.0 %layer.1 = bf16[64,512]{1,0:T(8,128)(2,1)} custom-call(s32[16]{0:T(128)} %len_ref.1, bf16[16,2048]{1,0:T(8,128)(2,1)} %q_hbm.1, bf16[16,128]{1,0:T(8,128)(2,1)} %nk_hbm.1, bf16[16,128]{1,0:T(8,128)(2,1)} %nv_hbm.1, bf16[64,512]{1,0:T(8,128)(2,1)} %res_hbm.1, f32[1,512]{1,0:T(1,128)} %bitcast.1, bf16[16,256,128]{2,1,0:T(8,128)(2,1)} %k_hbm.1, ...), custom_call_target="tpu_custom_call" | custom-call | tf_op jit(solution)/shard_map/layer/pallas_call | solution.py:481
  98.0 1.5 %copy.14 = bf16[64,512]{1,0:T(8,128)(2,1)} copy(bf16[64,512]{1,0:T(8,128)(2,1)} %layer.1) | data formatting | bytes 131072

commit v3 on v2

--- a/solution.py
+++ b/solution.py
@@ -23,9 +23,11 @@
     k_hbm, v_hbm, wo_hbm, wg_hbm, wu_hbm, wd_hbm,
     out_ref,
     q_ref, nk_ref, nv_ref, res_ref, gain_ref, kv, vv, wo, wg, wu, wd, gain_sib, qs, ao, ps, pr, ag, po, cs, cr, zs, zr, zt, st,
-    xn, sq, gs, gr, gp, gr2, ac, fin,
+    xn, sq, ga0, ga1, gb0, gb1, ra0, ra1, rb0, rb1, ha0, ha1, hb0, hb1, gp0, gp1, gr20, gr21, ac0, ac1, psum, scales, fin,
     lsem, wss, wrs, d2s, d2r, p4s, p4r, zss, zrs,
 ):
+    ga, gb, ra, rb = (ga0, ga1), (gb0, gb1), (ra0, ra1), (rb0, rb1)
+    ha, hb, gp, gr2, ac = (ha0, ha1), (hb0, hb1), (gp0, gp1), (gr20, gr21), (ac0, ac1)
     w = lax.axis_index("wide")
     z = lax.axis_index("narrow")
     c = lax.rem(w, 2)
@@ -191,27 +193,32 @@
 
     rows = NX * NY * 16
 
-    def project(s, k, buf, weight):
+    def project(s, k, buf, weight, first=0, last=True):
         depth_here = buf.shape[-1]
+        copy = None
         for half_index in (1, 0):
             for n in range(weight.shape[-1] // 256):
                 cols = slice(n * 256, (n + 1) * 256)
-                acc = jnp.dot(buf[s].reshape(rows, depth_here), weight[half_index, :, cols],
+                acc = jnp.dot(buf[s].reshape(rows, depth_here),
+                              weight[half_index, first:first + depth_here, cols],
                               preferred_element_type=F32)
                 for a in range(NY):
                     for b in range(NX):
                         r = (a * NX + b) * 16
                         to = pl.ds(pl.multiple_of(natural(a, b) * 16, 16), 16)
-                        if half_index:
-                            cs[s, k, to, cols] = acc[r:r + 16].astype(BF16)
+                        value = acc[r:r + 16]
+                        held = psum if half_index else po.at[s, k]
+                        if first:
+                            value = value + held[to, cols]
+                        if half_index and last:
+                            cs[s, k, to, cols] = value.astype(BF16)
                         else:
-                            po[s, k, to, cols] = acc[r:r + 16]
-            if half_index:
+                            held[to, cols] = value
+            if half_index and last:
                 copy = send(cs.at[s, k], cr.at[s, k], d2s.at[s, 1 + k], d2r.at[s, 1 + k], sibling)
         return copy
 
     share = rows // NZ
-
     top, bottom = slice(0, share // 2), slice(share // 2, share)
 
     def zsend(s, k, i, src, dst, d):
@@ -303,70 +310,118 @@
         return send(xn.at[s, :, :, 0:depth], xn.at[s, :, :, depth:2 * depth],
                     d2s.at[s, 3], d2r.at[s, 3], sibling)
 
-    def spread(s, cols, value):
+    parts = [(0, ac[0].shape[-1]), (ac[0].shape[-1], ac[1].shape[-1])]
+
+    def spread(buf, s, cols, value):
         for j in range(NY):
             for i in range(NX):
                 r = (j * NX + i) * 16
                 first = jnp.where(c == 0, i, j)
                 second = jnp.where(c == 0, j, i)
-                gs[s, first, second, :, cols] = value[r:r + 16]
-
-    def expand(s, copy):
+                buf[s, first, second, :, cols] = value[r:r + 16]
+
+    def expand(s, part):
+        base, count = parts[part]
+        for weight, buf in ((wg, ga[part]), (wu, gb[part])):
+            for start in range(0, count, 256):
+                size = min(256, count - start)
+                acc = jnp.dot(xn[s].reshape(rows, 2 * depth),
+                              weight[:, base + start:base + start + size],
+                              preferred_element_type=F32)
+                spread(buf, s, slice(start, start + size), acc.astype(BF16))
+
+    def plane_send(s, part, i, src, dst, d):
+        return send(src, dst, p4s.at[s, 2 + part, i], p4r.at[s, 2 + part, i], pdev(d))
+
+    def scatter_first(s, part):
+        a, b, ta, tb = ga[part], gb[part], ra[part], rb[part]
+        return [
+            plane_send(s, part, 0, a.at[s, ppeer(2)], ta.at[s, 0], 1),
+            plane_send(s, part, 1, b.at[s, ppeer(2)], tb.at[s, 0], 3),
+            plane_send(s, part, 2, a.at[s, ppeer(3)], ta.at[s, 1], 3),
+            plane_send(s, part, 3, b.at[s, ppeer(1)], tb.at[s, 1], 1),
+        ]
+
+    def add_rows(terms, count, out, base, squares_too):
+        def block(j, _):
+            blocks = [get(j) for get in terms]
+            acc = blocks[0][:, 0:count].astype(F32)
+            for value in blocks[1:]:
+                acc += value[:, 0:count].astype(F32)
+            out[j, :, base:base + count] = acc.astype(BF16)
+            if squares_too:
+                square = decode(blocks[0][:, count:])
+                for value in blocks[1:]:
+                    square += decode(value[:, count:])
+                end = out.shape[-1]
+                out[j, :, end - 128:end] = encode(square)
+            return 0
+        lax.fori_loop(0, NY, block, 0)
+
+    def relay(s, part, copies):
+        a, b, ta, tb = ga[part], gb[part], ra[part], rb[part]
+        count = parts[part][1]
+        copies[0].wait_recv()
+        add_rows([lambda j: a[s, ppeer(1), j], lambda j: ta[s, 0, j]], count,
+                 ha[part].at[s], 0, part == 0)
+        copies.append(plane_send(s, part, 4, ha[part].at[s], ta.at[s, 2], 1))
+        copies[1].wait_recv()
+        add_rows([lambda j: b[s, ppeer(3), j], lambda j: tb[s, 0, j]], count,
+                 hb[part].at[s], 0, False)
+        copies.append(plane_send(s, part, 5, hb[part].at[s], tb.at[s, 2], 3))
+        return copies[2:]
+
+    def scatter_second(s, part, copies):
+        a, b, ta, tb = ga[part], gb[part], ra[part], rb[part]
+        count = parts[part][1]
+        arrive(copies)
+        add_rows([lambda j: a[s, p, j], lambda j: ta[s, 1, j], lambda j: ta[s, 2, j]], count,
+                 gp[part].at[s], 0, part == 0)
+        add_rows([lambda j: b[s, p, j], lambda j: tb[s, 1, j], lambda j: tb[s, 2, j]], count,
+                 gp[part].at[s], count, False)
+        return [
+            send(gp[part].at[s, qpeer(d)], gr2[part].at[s, d - 1],
+                 p4s.at[s, 4 + part, d - 1], p4r.at[s, 4 + part, d - 1], qdev(d))
+            for d in (2, 1, 3)
+        ]
+
+    def activate(s, part, copies):
+        arrive(copies)
+        count = parts[part][1]
+        if part == 0:
+            square = decode(gp[0][s, q, :, 2 * count:])
+            for d in range(3):
+                square += decode(gr2[0][s, d, :, 2 * count:])
+            scales[s] = lax.rsqrt(square / D + EPS)
+        factor = scales[s]
+        for n in range(count // 128):
+            cols = slice(n * 128, (n + 1) * 128)
+            lift_cols = slice(count + n * 128, count + (n + 1) * 128)
+            gate = gp[part][s, q, :, cols].astype(F32)
+            lift = gp[part][s, q, :, lift_cols].astype(F32)
+            for d in range(3):
+                gate += gr2[part][s, d, :, cols].astype(F32)
+                lift += gr2[part][s, d, :, lift_cols].astype(F32)
+            gate = gate * factor
+            ac[part][s, q, p, :, cols] = (
+                gate / (1.0 + jnp.exp(-gate)) * (lift * factor)
+            ).astype(BF16)
+        return gather_first(s, 6 + part, ac[part])
+
+    def gather_on(s, part, copies):
+        arrive(copies)
+        return gather_second(s, 8 + part, ac[part])
+
+    def down(s, part, copies):
+        arrive(copies)
+        return project(s, 1, ac[part], wd, parts[part][0], part == 1)
+
+    def squares(s, copy):
         row_squares(s, 0)
         copy.wait_recv()
         row_squares(s, depth)
-        spread(s, slice(2 * units, 2 * units + 128), encode(sq[...]))
-        for k, weight in enumerate((wg, wu)):
-            for start in range(0, units, 256):
-                size = min(256, units - start)
-                acc = jnp.dot(xn[s].reshape(rows, 2 * depth), weight[:, start:start + size],
-                              preferred_element_type=F32)
-                base = k * units + start
-                spread(s, slice(base, base + size), acc.astype(BF16))
-        return [
-            send(gs.at[s, ppeer(d)], gr.at[s, d - 1], p4s.at[s, 2, d - 1], p4r.at[s, 2, d - 1],
-                 pdev(d))
-            for d in (2, 1, 3)
-        ]
-
-    def sum_second(s, copies):
-        arrive(copies)
-
-        def block(j, _):
-            acc = gs[s, p, j, :, 0:2 * units].astype(F32)
-            square = decode(gs[s, p, j, :, 2 * units:])
-            for d in range(3):
-                acc += gr[s, d, j, :, 0:2 * units].astype(F32)
-                square += decode(gr[s, d, j, :, 2 * units:])
-            gp[s, j, :, 0:2 * units] = acc.astype(BF16)
-            gp[s, j, :, 2 * units:] = encode(square)
-            return 0
-        lax.fori_loop(0, NY, block, 0)
-        return [
-            send(gp.at[s, qpeer(d)], gr2.at[s, d - 1], p4s.at[s, 3, d - 1], p4r.at[s, 3, d - 1],
-                 qdev(d))
-            for d in (2, 1, 3)
-        ]
-
-    def activate(s, copies):
-        arrive(copies)
-        square = decode(gp[s, q, :, 2 * units:])
-        for d in range(3):
-            square += decode(gr2[s, d, :, 2 * units:])
-        factor = lax.rsqrt(square / D + EPS)
-        for n in range(units // 128):
-            cols = slice(n * 128, (n + 1) * 128)
-            lift_cols = slice(units + n * 128, units + (n + 1) * 128)
-            gate = gp[s, q, :, cols].astype(F32)
-            lift = gp[s, q, :, lift_cols].astype(F32)
-            for d in range(3):
-                gate += gr2[s, d, :, cols].astype(F32)
-                lift += gr2[s, d, :, lift_cols].astype(F32)
-            gate = gate * factor
-            ac[s, q, p, :, cols] = (
-                gate / (1.0 + jnp.exp(-gate)) * (lift * factor)
-            ).astype(BF16)
-        return gather_first(s, 4, ac)
+        count = parts[0][1]
+        spread(ga[0], s, slice(count, count + 128), encode(sq[...]))
 
     S = range(STREAMS)
     for s in S:
@@ -400,25 +455,41 @@
     n1 = [relay_normed(s, n1[s]) for s in S]
     drain(32)
     share_wd.wait_recv()
-    e1 = []
-    for s in S:
-        e1.append(expand(s, swap_normed(s, n1[s])))
-    drain(48)
-    e2 = [sum_second(0, e1[0])]
-    b1 = [activate(0, e2[0])]
-    e2.append(sum_second(1, e1[1]))
-    arrive(b1[0])
-    b2 = [gather_second(0, 5, ac)]
-    b1.append(activate(1, e2[1]))
-    arrive(b2[0])
-    c2 = project(0, 1, ac, wd)
-    arrive(b1[1])
-    b2.append(gather_second(1, 5, ac))
+    squares(0, swap_normed(0, n1[0]))
+    expand(0, 0)
+    e1 = {(0, 0): scatter_first(0, 0)}
+    expand(0, 1)
+    e1[0, 1] = scatter_first(0, 1)
+    squares(1, swap_normed(1, n1[1]))
+    drain(40)
+    e2, f1, f2 = {}, {}, {}
+    e1[0, 0] = relay(0, 0, e1[0, 0])
+    expand(1, 0)
+    e1[0, 1] = relay(0, 1, e1[0, 1])
+    e1[1, 0] = scatter_first(1, 0)
+    expand(1, 1)
+    e2[0, 0] = scatter_second(0, 0, e1[0, 0])
+    e1[1, 1] = scatter_first(1, 1)
+    e2[0, 1] = scatter_second(0, 1, e1[0, 1])
+    e1[1, 0] = relay(1, 0, e1[1, 0])
+    f1[0, 0] = activate(0, 0, e2[0, 0])
+    e1[1, 1] = relay(1, 1, e1[1, 1])
+    f1[0, 1] = activate(0, 1, e2[0, 1])
+    e2[1, 0] = scatter_second(1, 0, e1[1, 0])
+    f2[0, 0] = gather_on(0, 0, f1[0, 0])
+    e2[1, 1] = scatter_second(1, 1, e1[1, 1])
+    f2[0, 1] = gather_on(0, 1, f1[0, 1])
+    f1[1, 0] = activate(1, 0, e2[1, 0])
+    f1[1, 1] = activate(1, 1, e2[1, 1])
+    down(0, 0, f2[0, 0])
+    f2[1, 0] = gather_on(1, 0, f1[1, 0])
+    f2[1, 1] = gather_on(1, 1, f1[1, 1])
+    c2 = down(0, 1, f2[0, 1])
     r2 = [scatter_z(0, 1, c2)]
-    drain(len(sent) - 24)
-    arrive(b2[1])
-    c2 = project(1, 1, ac, wd)
+    drain(len(sent) - 30)
+    down(1, 0, f2[1, 0])
     r2[0] = relay_z(0, 1, r2[0])
+    c2 = down(1, 1, f2[1, 1])
     r2.append(scatter_z(1, 1, c2))
     drain(len(sent) - 16)
     r2[1] = relay_z(1, 1, r2[1])
@@ -442,7 +513,8 @@
     cols = out_weight.shape[1]
     depth, hidden = gate_weight.shape
     units = hidden // 2
-    wide_row = 2 * units + 128
+    cut = units // 256 * 128
+    w0, w1 = 2 * cut + 128, 2 * (units - cut)
     rows = NX * NY * 2 * half
     share = rows // NZ
     S = STREAMS
@@ -467,13 +539,20 @@
         v(S, 2, 2, share, cols),
         v(S, share, cols, dtype=F32),
         v(S, NZ, share, 2 * depth), v(rows, 128, dtype=F32),
-        v(S, NX, NY, 16, wide_row), v(S, 3, NY, 16, wide_row),
-        v(S, NY, 16, wide_row), v(S, 3, 16, wide_row),
-        v(S, NY, NX, 16, units),
+        v(S, NX, NY, 16, cut + 128), v(S, NX, NY, 16, units - cut),
+        v(S, NX, NY, 16, cut), v(S, NX, NY, 16, units - cut),
+        v(S, 3, NY, 16, cut + 128), v(S, 3, NY, 16, units - cut),
+        v(S, 3, NY, 16, cut), v(S, 3, NY, 16, units - cut),
+        v(S, NY, 16, cut + 128), v(S, NY, 16, units - cut),
+        v(S, NY, 16, cut), v(S, NY, 16, units - cut),
+        v(S, NY, 16, w0), v(S, NY, 16, w1),
+        v(S, 3, 16, w0), v(S, 3, 16, w1),
+        v(S, NY, NX, 16, cut), v(S, NY, NX, 16, units - cut),
+        v(rows, cols, dtype=F32), v(S, 16, 128, dtype=F32),
         v(S, share, cols, dtype=F32),
         DMA((13,)), DMA((5,)), DMA((5,)),
         DMA((S, 4)), DMA((S, 4)),
-        DMA((S, 6, 3)), DMA((S, 6, 3)),
+        DMA((S, 10, 6)), DMA((S, 10, 6)),
         DMA((S, 3, 8)), DMA((S, 3, 8)),
     ]
     vm = pl.BlockSpec(memory_space=pltpu.VMEM)

time: 99.6 us -> 92.7 us (0.931)
  Pallas kernels: 98 us -> 91.1 us
    pallas_call x1, Pallas kernels: 98 us -> 91.1 us  [local(): pl.pallas_call(body, out_shape=jax.ShapeDtypeStruct(residual.shape, BF16)...]
where the time goes in v3:
time: 92.7 us; the launch traced here: 92.6 us
  Pallas kernels  91.1 us (98%)
  local copies, waits for them, and re-layouts  1.47 us (2%)
    pallas_call x1, Pallas kernels, local(): pl.pallas_call(body, out_shape=jax.ShapeDtypeStruct(residual.shape, BF16)...  91.1 us

profile of v3, /device:TPU:1, one launch (start us, length us, event | category | flops | bytes accessed | tf_op | source)
XLA Modules:
  0.0 92.6 jit_solution(9619235694583815119)
XLA Ops:
  0.0 91.1 %layer.1 = bf16[64,512]{1,0:T(8,128)(2,1)} custom-call(s32[16]{0:T(128)} %len_ref.1, bf16[16,2048]{1,0:T(8,128)(2,1)} %q_hbm.1, bf16[16,128]{1,0:T(8,128)(2,1)} %nk_hbm.1, bf16[16,128]{1,0:T(8,128)(2,1)} %nv_hbm.1, bf16[64,512]{1,0:T(8,128)(2,1)} %res_hbm.1, f32[1,512]{1,0:T(1,128)} %bitcast.1, bf16[16,256,128]{2,1,0:T(8,128)(2,1)} %k_hbm.1, ...), custom_call_target="tpu_custom_call" | custom-call | tf_op jit(solution)/shard_map/layer/pallas_call | solution.py:560
  91.1 1.5 %copy.14 = bf16[64,512]{1,0:T(8,128)(2,1)} copy(bf16[64,512]{1,0:T(8,128)(2,1)} %layer.1) | data formatting | bytes 131072

commit v4 on v3

--- a/solution.py
+++ b/solution.py
@@ -177,6 +177,21 @@
             for d in (2, 1, 3)
         ]
 
+    low, high = slice(0, NX // 2), slice(NX // 2, NX)
+
+    def gather_around(s, k, buf):
+        return [
+            send(buf.at[s, q, part], buf.at[s, q, part], p4s.at[s, k, i], p4r.at[s, k, i], qdev(d))
+            for i, (part, d) in enumerate(((low, 1), (high, 3), (high, 1), (low, 3)))
+        ]
+
+    def forward(s, k, buf, copies):
+        for i, (part, d) in enumerate(((low, 1), (high, 3))):
+            copies[i].wait_recv()
+            block = buf.at[s, qpeer(4 - d), part]
+            copies.append(send(block, block, p4s.at[s, k, 4 + i], p4r.at[s, k, 4 + i], qdev(d)))
+        return copies[2:]
+
     def arrive(copies):
         for copy in copies:
             copy.wait_recv()
@@ -410,7 +425,7 @@
 
     def gather_on(s, part, copies):
         arrive(copies)
-        return gather_second(s, 8 + part, ac[part])
+        return gather_around(s, 8 + part, ac[part])
 
     def down(s, part, copies):
         arrive(copies)
@@ -480,13 +495,17 @@
     e2[1, 1] = scatter_second(1, 1, e1[1, 1])
     f2[0, 1] = gather_on(0, 1, f1[0, 1])
     f1[1, 0] = activate(1, 0, e2[1, 0])
+    f2[0, 0] = forward(0, 8, ac[0], f2[0, 0])
     f1[1, 1] = activate(1, 1, e2[1, 1])
-    down(0, 0, f2[0, 0])
+    f2[0, 1] = forward(0, 9, ac[1], f2[0, 1])
     f2[1, 0] = gather_on(1, 0, f1[1, 0])
     f2[1, 1] = gather_on(1, 1, f1[1, 1])
+    down(0, 0, f2[0, 0])
     c2 = down(0, 1, f2[0, 1])
+    f2[1, 0] = forward(1, 8, ac[0], f2[1, 0])
     r2 = [scatter_z(0, 1, c2)]
-    drain(len(sent) - 30)
+    f2[1, 1] = forward(1, 9, ac[1], f2[1, 1])
+    drain(len(sent) - 40)
     down(1, 0, f2[1, 0])
     r2[0] = relay_z(0, 1, r2[0])
     c2 = down(1, 1, f2[1, 1])

time: 92.7 us -> 91.7 us (0.989)
  Pallas kernels: 91.1 us -> 90 us
    pallas_call x1, Pallas kernels: 91.1 us -> 90 us  [local(): pl.pallas_call(body, out_shape=jax.ShapeDtypeStruct(residual.shape, BF16)...]
where the time goes in v4:
time: 91.7 us; the launch traced here: 91.5 us
  Pallas kernels  90 us (98%)
  local copies, waits for them, and re-layouts  1.47 us (2%)
    pallas_call x1, Pallas kernels, local(): pl.pallas_call(body, out_shape=jax.ShapeDtypeStruct(residual.shape, BF16)...  90 us

profile of v4, /device:TPU:1, one launch (start us, length us, event | category | flops | bytes accessed | tf_op | source)
XLA Modules:
  0.0 91.5 jit_solution(1203923671469918761)
XLA Ops:
  0.0 90.0 %layer.1 = bf16[64,512]{1,0:T(8,128)(2,1)} custom-call(s32[16]{0:T(128)} %len_ref.1, bf16[16,2048]{1,0:T(8,128)(2,1)} %q_hbm.1, bf16[16,128]{1,0:T(8,128)(2,1)} %nk_hbm.1, bf16[16,128]{1,0:T(8,128)(2,1)} %nv_hbm.1, bf16[64,512]{1,0:T(8,128)(2,1)} %res_hbm.1, f32[1,512]{1,0:T(1,128)} %bitcast.1, bf16[16,256,128]{2,1,0:T(8,128)(2,1)} %k_hbm.1, ...), custom_call_target="tpu_custom_call" | custom-call | tf_op jit(solution)/shard_map/layer/pallas_call | solution.py:579
  90.0 1.5 %copy.14 = bf16[64,512]{1,0:T(8,128)(2,1)} copy(bf16[64,512]{1,0:T(8,128)(2,1)} %layer.1) | data formatting | bytes 131072

commit v5 on v4

--- a/solution.py
+++ b/solution.py
@@ -335,9 +335,10 @@
                 second = jnp.where(c == 0, j, i)
                 buf[s, first, second, :, cols] = value[r:r + 16]
 
-    def expand(s, part):
+    def expand(s, part, which=(0, 1)):
         base, count = parts[part]
-        for weight, buf in ((wg, ga[part]), (wu, gb[part])):
+        for k in which:
+            weight, buf = ((wg, ga[part]), (wu, gb[part]))[k]
             for start in range(0, count, 256):
                 size = min(256, count - start)
                 acc = jnp.dot(xn[s].reshape(rows, 2 * depth),
@@ -349,11 +350,21 @@
         return send(src, dst, p4s.at[s, 2 + part, i], p4r.at[s, 2 + part, i], pdev(d))
 
     def scatter_first(s, part):
-        a, b, ta, tb = ga[part], gb[part], ra[part], rb[part]
+        first = scatter_gate(s, part)
+        second = scatter_up(s, part)
+        return [first[0], second[0], first[1], second[1]]
+
+    def scatter_gate(s, part):
+        a, ta = ga[part], ra[part]
         return [
             plane_send(s, part, 0, a.at[s, ppeer(2)], ta.at[s, 0], 1),
+            plane_send(s, part, 2, a.at[s, ppeer(3)], ta.at[s, 1], 3),
+        ]
+
+    def scatter_up(s, part):
+        b, tb = gb[part], rb[part]
+        return [
             plane_send(s, part, 1, b.at[s, ppeer(2)], tb.at[s, 0], 3),
-            plane_send(s, part, 2, a.at[s, ppeer(3)], ta.at[s, 1], 3),
             plane_send(s, part, 3, b.at[s, ppeer(1)], tb.at[s, 1], 1),
         ]
 
@@ -471,10 +482,13 @@
     drain(32)
     share_wd.wait_recv()
     squares(0, swap_normed(0, n1[0]))
-    expand(0, 0)
-    e1 = {(0, 0): scatter_first(0, 0)}
-    expand(0, 1)
-    e1[0, 1] = scatter_first(0, 1)
+    e1 = {}
+    for part in (0, 1):
+        expand(0, part, (0,))
+        first = scatter_gate(0, part)
+        expand(0, part, (1,))
+        second = scatter_up(0, part)
+        e1[0, part] = [first[0], second[0], first[1], second[1]]
     squares(1, swap_normed(1, n1[1]))
     drain(40)
     e2, f1, f2 = {}, {}, {}

time: 91.7 us -> 94.1 us (1.026)
  Pallas kernels: 90 us -> 92.5 us
    pallas_call x1, Pallas kernels: 90 us -> 92.5 us  [local(): pl.pallas_call(body, out_shape=jax.ShapeDtypeStruct(residual.shape, BF16)...]
where the time goes in v5:
time: 94.1 us; the launch traced here: 94 us
  Pallas kernels  92.5 us (98%)
  local copies, waits for them, and re-layouts  1.47 us (2%)
    pallas_call x1, Pallas kernels, local(): pl.pallas_call(body, out_shape=jax.ShapeDtypeStruct(residual.shape, BF16)...  92.5 us

profile of v5, /device:TPU:1, one launch (start us, length us, event | category | flops | bytes accessed | tf_op | source)
XLA Modules:
  0.0 94.0 jit_solution(3565815744317879419)
XLA Ops:
  0.0 92.5 %layer.1 = bf16[64,512]{1,0:T(8,128)(2,1)} custom-call(s32[16]{0:T(128)} %len_ref.1, bf16[16,2048]{1,0:T(8,128)(2,1)} %q_hbm.1, bf16[16,128]{1,0:T(8,128)(2,1)} %nk_hbm.1, bf16[16,128]{1,0:T(8,128)(2,1)} %nv_hbm.1, bf16[64,512]{1,0:T(8,128)(2,1)} %res_hbm.1, f32[1,512]{1,0:T(1,128)} %bitcast.1, bf16[16,256,128]{2,1,0:T(8,128)(2,1)} %k_hbm.1, ...), custom_call_target="tpu_custom_call" | custom-call | tf_op jit(solution)/shard_map/layer/pallas_call | solution.py:593
  92.5 1.5 %copy.14 = bf16[64,512]{1,0:T(8,128)(2,1)} copy(bf16[64,512]{1,0:T(8,128)(2,1)} %layer.1) | data formatting | bytes 131072
